TPU v7x, 512 devices: a whole 4x4x16 slice. The times are simulated.
512 devices in a mesh: rows: 64 (over z, x_hi, core), feat: 8 (over y, x_lo).
Axes of the slice: x: 4 (x_hi: 2, x_lo: 2; x = x_hi * 2 + x_lo), y: 4, z: 16, core: 2. Of those that a mesh axis runs over, the one named last changes fastest.
Arguments:
- gradients: bfloat16 [65536, 8192], P('rows', 'feat'), may hold values from -2500 to 2500
- queries: bfloat16 [1024, 8192], P('rows', 'feat'), may hold values from -0.1875 to 0.1875
- loss_weight: float32 [65536], P('rows'), may hold values from 0.09 to 1
Outputs:
- standardized: bfloat16 [65536, 1024], P('rows', 'feat')
All inputs are finite; a program needn't handle non-finite values.
Results may differ from a plain program's by a relative error of at most 0.019.
Values may be sent and summed in bfloat16 or wider, within the bound.
A program may use at most 64 MiB of HBM per device.

v0:
```python
import jax
import jax.numpy as jnp
from jax import lax
from jax.sharding import PartitionSpec as P

NORM_EPS = 1e-06
VAR_EPS = 1e-05


def body(gradients, queries, loss_weight):
    rows_here = gradients.shape[0]
    total_rows = rows_here * lax.axis_size("rows")
    feature_count = gradients.shape[1] * lax.axis_size("feat")
    local_squares = jnp.sum(jnp.square(gradients.astype(jnp.float32)), axis=1)
    squares = lax.psum(local_squares, "feat")
    product = lax.dot_general(
        gradients,
        lax.all_gather(queries, "rows", axis=0, tiled=True),
        (((1,), (1,)), ((), ())),
        preferred_element_type=jnp.float32,
    )
    partial_value = product.astype(jnp.bfloat16)
    partial_float = partial_value.astype(jnp.float32)
    query_share = partial_value.shape[1] // lax.axis_size("feat")
    summed = lax.psum(partial_float.astype(jnp.bfloat16), "feat").astype(jnp.float32)
    raw = lax.dynamic_slice_in_dim(summed, lax.axis_index("feat") * query_share, query_share, 1)
    factor = loss_weight / jnp.sqrt(squares / feature_count + NORM_EPS)
    scored = raw * factor[:, None]
    sums = lax.psum(jnp.sum(scored, axis=0), "rows")
    column_mean = sums / total_rows
    centered = scored - column_mean[None, :]
    square_sums = lax.psum(jnp.sum(centered * centered, axis=0), "rows")
    column_var = square_sums / total_rows
    return (centered * lax.rsqrt(column_var + VAR_EPS)[None, :]).astype(jnp.bfloat16)


def solution(mesh):
    in_specs = (P("rows", "feat"), P("rows", "feat"), P("rows"))
    out_specs = P("rows", "feat")
    return jax.shard_map(body, mesh=mesh, in_specs=in_specs, out_specs=out_specs, check_vma=False)
```

profile of v0, /device:TPU:1, one launch (start us, length us, event | category | flops | bytes accessed | tf_op | source)
XLA Modules:
  0.0 554.2 jit_solution(9784437294390381121)
XLA Ops:
  6.5 0.0 all-gather.2.cloned.1.call-start
  6.5 0.7 all-gather.2.cloned.1.call-update
  7.3 0.0 all-reduce.2.cloned.1.call-start
  7.3 152.9 %all-gather.2.cloned.1.call-done = bf16[1024,1024]{1,0:T(8,128)(2,1)} async-done(((bf16[16,1024]{1,0:T(8,128)(2,1)}), bf16[1024,1024]{1,0:T(8,128)(2,1)}) %all-gather.2.cloned.1.call-update) | async-done | bytes 2097168 | tf_op jit(solution)/shard_map/all_gather | solution.py:18
  160.2 5.9 %convolution_convert_fusion = bf16[1024,1024]{1,0:T(8,128)(2,1)} fusion(bf16[1024,1024]{1,0:T(8,128)(2,1)} %param.3, bf16[1024,1024]{1,0:T(8,128)(2,1)} %all-gather.2.cloned.1.call-done), kind=kOutput, calls=%fused_computation.1 | convolution fusion | flops 2148532224 | bytes 6291456 | tf_op jit(solution)/shard_map/dot_general | solution.py:16
  166.1 0.0 copy-start
  166.1 0.0 copy-start.1
  166.1 0.0 all-reduce.2.cloned.1.call-update
  166.2 1.6 copy-done
  167.7 0.5 multiply_reduce_fusion
  168.2 15.4 %psum.29 = f32[1024]{0:T(1024)S(1)} all-reduce(f32[1024]{0:T(1024)S(1)} %multiply_reduce_fusion), channel_id=1, replica_groups=mesh['rows'=64,'feat'=8] {'feat'}, use_global_device_ids=true, to_apply=%region_2.0 | all-reduce | flops 1024 | bytes 8192 | tf_op jit(solution)/shard_map/psum | solution.py:15
  183.6 0.0 copy-done.1
  183.6 96.5 %all-reduce.2.cloned.1.call-done = bf16[1024,1024]{1,0:T(8,128)(2,1)} async-done(((bf16[1024,1024]{1,0:T(8,128)(2,1)}), bf16[1024,1024]{1,0:T(8,128)(2,1)}) %all-reduce.2.cloned.1.call-update) | async-done | bytes 2097168 | tf_op jit(solution)/shard_map/psum | solution.py:25
  280.1 1.2 fusion.1
  281.2 129.9 %psum.30 = f32[128]{0:T(128)S(1)} all-reduce(f32[128]{0:T(128)S(1)} %fusion.1), channel_id=1, replica_groups=mesh['rows'=64,'feat'=8] {'rows'}, use_global_device_ids=true, to_apply=%region_4.0 | all-reduce | flops 128 | bytes 1024 | tf_op jit(solution)/shard_map/psum | solution.py:29
  411.2 1.2 multiply_reduce_fusion.1
  412.3 133.2 %psum.31 = f32[128]{0:T(128)S(1)} all-reduce(f32[128]{0:T(128)S(1)} %multiply_reduce_fusion.1), channel_id=1, replica_groups=mesh['rows'=64,'feat'=8] {'rows'}, use_global_device_ids=true, to_apply=%region_6.0 | all-reduce | flops 128 | bytes 1024 | tf_op jit(solution)/shard_map/psum | solution.py:32
  545.5 1.9 multiply_convert_fusion
  (3 shorter events, 0.0 us)
Async XLA Ops:
  6.5 153.6 %all-gather.2.cloned.1.call-start = ((), (), s32[]{:S(2)}) async-start(), calls=%async_computation | async-start | bytes 2129920 | tf_op jit(solution)/shard_map/all_gather | solution.py:18
  7.3 272.8 %all-reduce.2.cloned.1.call-start = ((), (), s32[]{:S(2)}) async-start(), calls=%async_computation.1 | async-start | bytes 4194304 | tf_op jit(solution)/shard_map/psum | solution.py:25
  166.1 1.6 copy-start
  166.1 17.4 %copy-start.1 = (f32[1024]{0:T(1024)S(1)}, f32[1024]{0:T(1024)}, u32[]{:S(2)}) copy-start(f32[1024]{0:T(1024)} %param.5) | copy-start | bytes 12292
Sparse Core Ops, SparseCore 0:
  10.6 149.4 all-gather.1
  166.3 113.7 all-reduce.1
where the time goes:
time: 555 us; the launch traced here: 554 us
  blocking collectives  278 us (50%)
  waiting for transfers between devices  250 us (45%)
  between operations  13.4 us (2%)
  matrix products  5.94 us (1%)
    all_gather x1, waiting for transfers between devices, body(): lax.all_gather(queries, 'rows', axis=0, tiled=True)  153 us
    psum x1, blocking collectives, body(): square_sums = lax.psum(jnp.sum(centered * centered, axis=0), 'rows')  133 us
    psum x1, blocking collectives, body(): sums = lax.psum(jnp.sum(scored, axis=0), 'rows')  130 us
    psum x1, waiting for transfers between devices, body(): lax.psum(partial_float.astype(jnp.bfloat16), 'feat').astype(jnp.float32)  96.5 us
    psum x1, blocking collectives, body(): squares = lax.psum(local_squares, 'feat')  15.4 us
  transfers between devices with their start and end apart: 2, of which 2 were waited for; matrix products, arithmetic and copies ran while one was open for 0% of the time, Pallas kernels for 0%

commit v1 on v0

--- a/solution.py
+++ b/solution.py
@@ -15,7 +15,9 @@
     squares = lax.psum(local_squares, "feat")
     product = lax.dot_general(
         gradients,
-        lax.all_gather(queries, "rows", axis=0, tiled=True),
+        jnp.concatenate(
+            lax.all_to_all(jnp.stack([queries] * lax.axis_size("rows")), "rows", 0, 0), axis=0
+        ),
         (((1,), (1,)), ((), ())),
         preferred_element_type=jnp.float32,
     )

time: 555 us -> 517 us (0.932)
  waiting for transfers between devices: 250 us -> 97.9 us
  blocking collectives: 278 us -> 396 us
    all_gather x1 -> x0, waiting for transfers between devices: 153 us -> none  [body(): lax.all_gather(queries, 'rows', axis=0, tiled=True)]
    all_to_all x0 -> x1, blocking collectives: none -> 118 us  [body(): lax.all_to_all(jnp.stack([queries] * lax.axis_size('rows')), 'rows', 0, 0)]
  transfers between devices with their start and end apart: 2 -> 1, of which waited for: 2 -> 1; matrix products, arithmetic and copies ran while one was open for 0% -> 0% of each run, Pallas kernels for 0% -> 0%
where the time goes in v1:
time: 517 us
  blocking collectives  396 us (77%)
  waiting for transfers between devices  97.9 us (19%)
  between operations  13.4 us (3%)
    psum x1, blocking collectives, body(): square_sums = lax.psum(jnp.sum(centered * centered, axis=0), 'rows')  133 us
    psum x1, blocking collectives, body(): sums = lax.psum(jnp.sum(scored, axis=0), 'rows')  130 us
    all_to_all x1, blocking collectives, body(): lax.all_to_all(jnp.stack([queries] * lax.axis_size('rows')), 'rows', 0, 0)  118 us
    psum x1, waiting for transfers between devices, body(): lax.psum(partial_float.astype(jnp.bfloat16), 'feat').astype(jnp.float32)  97.9 us
    psum x1, blocking collectives, body(): squares = lax.psum(local_squares, 'feat')  15.3 us
  transfers between devices with their start and end apart: 1, of which 1 were waited for; matrix products, arithmetic and copies ran while one was open for 0% of the time, Pallas kernels for 0%

profile of v1, /device:TPU:1, one launch (start us, length us, event | category | flops | bytes accessed | tf_op | source)
XLA Modules:
  0.0 517.0 jit_solution(17493297485773613622)
XLA Ops:
  6.5 0.0 all-reduce.2.cloned.1.call-start
  6.5 1.0 stack.2
  7.6 0.0 copy-start
  7.6 117.9 %all_to_all.5 = bf16[64,16,1024]{2,1,0:T(8,128)(2,1)S(1)} all-to-all(bf16[64,16,1024]{2,1,0:T(8,128)(2,1)S(1)} %stack.2), channel_id=1, replica_groups=mesh['rows'=64,'feat'=8] {'rows'}, dimensions={0} | all-to-all | bytes 4194304 | tf_op jit(solution)/shard_map/all_to_all | solution.py:19
  125.4 0.0 copy-done
  125.5 3.7 convolution_convert_fusion
  129.1 0.0 copy-start.1
  129.1 0.0 all-reduce.2.cloned.1.call-update
  129.2 0.5 multiply_reduce_fusion
  129.6 15.3 %psum.29 = f32[1024]{0:T(1024)S(1)} all-reduce(f32[1024]{0:T(1024)S(1)} %multiply_reduce_fusion), channel_id=1, replica_groups=mesh['rows'=64,'feat'=8] {'feat'}, use_global_device_ids=true, to_apply=%region_2.0 | all-reduce | flops 1024 | bytes 8192 | tf_op jit(solution)/shard_map/psum | solution.py:15
  145.0 0.0 copy-done.1
  145.0 97.9 %all-reduce.2.cloned.1.call-done = bf16[1024,1024]{1,0:T(8,128)(2,1)} async-done(((bf16[1024,1024]{1,0:T(8,128)(2,1)}), bf16[1024,1024]{1,0:T(8,128)(2,1)}) %all-reduce.2.cloned.1.call-update) | async-done | bytes 2097168 | tf_op jit(solution)/shard_map/psum | solution.py:27
  242.8 1.2 fusion.1
  244.0 129.9 %psum.30 = f32[128]{0:T(128)S(1)} all-reduce(f32[128]{0:T(128)S(1)} %fusion.1), channel_id=1, replica_groups=mesh['rows'=64,'feat'=8] {'rows'}, use_global_device_ids=true, to_apply=%region_4.0 | all-reduce | flops 128 | bytes 1024 | tf_op jit(solution)/shard_map/psum | solution.py:31
  373.9 1.2 multiply_reduce_fusion.1
  375.1 133.2 %psum.31 = f32[128]{0:T(128)S(1)} all-reduce(f32[128]{0:T(128)S(1)} %multiply_reduce_fusion.1), channel_id=1, replica_groups=mesh['rows'=64,'feat'=8] {'rows'}, use_global_device_ids=true, to_apply=%region_6.0 | all-reduce | flops 128 | bytes 1024 | tf_op jit(solution)/shard_map/psum | solution.py:34
  508.3 1.9 multiply_convert_fusion
  (3 shorter events, 0.0 us)
Async XLA Ops:
  6.5 236.3 %all-reduce.2.cloned.1.call-start = ((), (), s32[]{:S(2)}) async-start(), calls=%async_computation.1 | async-start | bytes 4194304 | tf_op jit(solution)/shard_map/psum | solution.py:27
  7.6 117.9 %copy-start = (bf16[1024,1024]{1,0:T(8,128)(2,1)S(1)}, bf16[1024,1024]{1,0:T(8,128)(2,1)}, u32[]{:S(2)}) copy-start(bf16[1024,1024]{1,0:T(8,128)(2,1)} %param.3) | copy-start | bytes 6291460
  129.1 15.8 %copy-start.1 = (f32[1024]{0:T(1024)S(1)}, f32[1024]{0:T(1024)}, u32[]{:S(2)}) copy-start(f32[1024]{0:T(1024)} %param.5) | copy-start | bytes 12292
Sparse Core Ops, SparseCore 0:
  129.3 113.5 all-reduce.1
